TPU v7x, 32 devices: a whole 2x2x4 slice. The times are simulated.
32 devices in a mesh: group: 2 (over x), run: 2 (over core), shard: 8 (over z, y).
Axes of the slice: x: 2, y: 2, z: 4, core: 2. Of those that a mesh axis runs over, the one named last changes fastest.
Arguments:
- weight: float32 [8, 4096, 512], P(('group', 'run'), 'shard'), parts along dimension 0, may hold values from -6 to 6
- first_moment: float32 [8, 4096, 512], P(('group', 'run'), 'shard'), parts along dimension 0, may hold values from -6 to 6
- second_moment: float32 [8, 4096, 512], P(('group', 'run'), 'shard'), parts along dimension 0, may hold values from 0.5 to 4
- norm_gain: float32 [8, 4096], P(('group', 'run')), parts along dimension 0, may hold values from 0.25 to 1.75
- learning_rate: float32 [8], P(('group', 'run')), parts along dimension 0, may hold values from 0.05 to 0.3
- momentum: float32 [8], P(('group', 'run')), parts along dimension 0, may hold values from 0.8 to 0.95
- inputs: bfloat16 [8, 6144, 4096], P(('group', 'run'), 'shard'), parts along dimension 0, may hold values from -6 to 6
- cotangent: bfloat16 [8, 6144, 512], P(('group', 'run'), 'shard'), parts along dimension 0, may hold values from -6 to 6
- winner: int32 [8], P('group'), parts along dimension 0, may hold values from 0 to 3, as said below
- perturb: int32 [8, 2], P('group'), parts along dimension 0, may hold values from 0 to 1
Outputs:
- keys: bfloat16 [8, 6144, 512], P(('group', 'run'), 'shard'), parts along dimension 0
- new_weight: float32 [8, 4096, 512], P(('group', 'run'), 'shard'), parts along dimension 0
- new_first: float32 [8, 4096, 512], P(('group', 'run'), 'shard'), parts along dimension 0
- new_second: float32 [8, 4096, 512], P(('group', 'run'), 'shard'), parts along dimension 0
- new_hyper: float32 [8, 2], P(('group', 'run')), parts along dimension 0
There are 2 independent parts, one for each index of `group`. A program takes and returns all parts, laid end to end along the dimension named above; each array names one. Nothing has to cross between parts.
Inputs may be any that keep to these rules, and one draw needn't show every extreme that they name: `winner`: 2 runs name themselves; every other run names one of those.
All inputs are finite; a program needn't handle non-finite values.
Results may differ from a plain program's by a relative error of at most 0.0058.
Values may be sent and summed in bfloat16 or wider, within the bound.
A program may use at most 192 MiB of HBM per device.

v0:
```python
import jax
import jax.numpy as jnp
from jax import lax
from jax.sharding import PartitionSpec as P


def per_device(
    weight,
    first_moment,
    second_moment,
    norm_gain,
    learning_rate,
    momentum,
    inputs,
    cotangent,
    winner,
    perturb,
):
    run_count = weight.shape[0]
    features = inputs.shape[2]
    offset = lax.axis_index("run") * run_count
    mine = offset + jnp.arange(run_count, dtype=jnp.int32)
    everyone = (
        lax.all_gather(weight, "run", axis=0, tiled=True),
        lax.all_gather(first_moment, "run", axis=0, tiled=True),
        lax.all_gather(second_moment, "run", axis=0, tiled=True),
        lax.all_gather(norm_gain, "run", axis=0, tiled=True),
        lax.all_gather(learning_rate, "run", axis=0, tiled=True),
        lax.all_gather(momentum, "run", axis=0, tiled=True),
    )
    source = lax.dynamic_slice(winner, (offset,), (run_count,))
    taken_weight, taken_first, taken_second, taken_gain, taken_rate, taken_momentum = [
        jnp.take(member, source, axis=0) for member in everyone
    ]
    loser = source != mine
    codes = lax.dynamic_slice(perturb, (offset, jnp.int32(0)), (run_count, 2))
    factor = jnp.where(codes == 0, jnp.float32(0.8), jnp.float32(1.25))
    factor = jnp.where(loser[:, None], factor, jnp.float32(1.0))
    rate = taken_rate * factor[:, 0]
    beta = 1.0 - (1.0 - taken_momentum) * factor[:, 1]
    values = inputs.astype(jnp.float32)
    square = jnp.mean(values * values, axis=-1, keepdims=True)
    normed = (values * lax.rsqrt(square + 1e-05) * taken_gain[:, None, :]).astype(jnp.bfloat16)
    wide = taken_weight.astype(jnp.bfloat16)
    scale = features ** (-0.5)
    columns = normed
    key_total = jnp.einsum(
        "rtd,rdk->rtk",
        columns,
        lax.all_gather(wide, "shard", axis=1, tiled=True),
        preferred_element_type=jnp.float32,
    )
    columns = normed
    grad_share = lax.psum_scatter(
        (
            jnp.einsum("rtd,rtk->drk", columns, cotangent, preferred_element_type=jnp.float32)
            * scale
        ).astype(jnp.bfloat16),
        "shard",
        scatter_dimension=0,
        tiled=True,
    ).astype(jnp.float32)
    grad = jnp.transpose(grad_share, (1, 0, 2))
    keys = (key_total * scale).astype(jnp.bfloat16)
    beta_full = beta[:, None, None]
    new_first = beta_full * taken_first + (1.0 - beta_full) * grad
    new_second = 0.95 * taken_second + 0.05 * grad * grad
    new_weight = taken_weight - rate[:, None, None] * new_first / (jnp.sqrt(new_second) + 1e-08)
    new_hyper = jnp.stack([rate, beta], axis=1)
    return (keys, new_weight, new_first, new_second, new_hyper)


def solution(mesh):
    placed = (
        P(("group", "run"), "shard", None),
        P(("group", "run"), "shard", None),
        P(("group", "run"), "shard", None),
        P(("group", "run"), None),
        P(("group", "run")),
        P(("group", "run")),
        P(("group", "run"), "shard", None),
        P(("group", "run"), "shard", None),
        P("group"),
        P("group", None),
    )
    return jax.shard_map(
        per_device,
        mesh=mesh,
        in_specs=placed,
        out_specs=(
            P(("group", "run"), "shard", None),
            P(("group", "run"), "shard", None),
            P(("group", "run"), "shard", None),
            P(("group", "run"), "shard", None),
            P(("group", "run"), None),
        ),
        check_vma=False,
    )
```

profile of v0, /device:TPU:0, one launch (start us, length us, event | category | flops | bytes accessed | tf_op | source)
XLA Modules:
  0.0 289.6 jit_solution(2750776347986622596)
XLA Ops:
  8.0 0.0 copy-start
  8.0 0.0 all-gather.6.cloned.1.call-start
  8.1 0.7 all-gather.6.cloned.1.call-update
  8.7 0.0 copy-start.1
  8.8 0.0 copy-start.3
  8.8 0.0 all-gather.10.cloned.1.call-start
  8.8 0.7 all-gather.10.cloned.1.call-update
  9.5 0.0 all-gather.12.cloned.1.call-start
  9.6 0.7 all-gather.12.cloned.1.call-update
  10.3 0.0 reduce-scatter.2.cloned.1.call-start
  10.3 0.0 copy-done.1
  10.3 2.0 all-gather
  12.3 0.1 reshape.112
  12.3 0.0 copy-done.3
  12.3 0.1 compare_and_fusion
  12.4 0.6 gather_fusion
  13.0 7.1 %fusion = f32[2,768]{1,0:T(2,128)S(1)} fusion(bf16[2,768,4096]{2,1,0:T(8,128)(2,1)} %param.20), kind=kLoop, calls=%fused_computation.8 | loop fusion | flops 18872832 | bytes 12589056 | tf_op jit(solution)/shard_map/reduce_sum | solution.py:42
  20.1 0.1 broadcast_select_fusion
  20.2 0.0 copy-done
  20.2 13.6 %fusion.7 = bf16[4096,2,512]{2,0,1:T(8,128)(2,1)} fusion(bf16[2,768,512]{2,1,0:T(8,128)(2,1)S(1)} %copy-done, bf16[2,768,4096]{2,1,0:T(8,128)(2,1)} %param.20, f32[2,4096]{1,0:T(2,128)S(1)} %broadcast_select_fusion, f32[2,768]{1,0:T(2,128)S(1)} %add_rsqrt_fusion), kind=kOutput, calls=%fused_computation.14 | convolution fusion | flops 6476005376 | bytes 22583296 | tf_op jit(solution)/shard_map/rtd,rtk->drk/dot_general | solution.py:56
  33.8 0.0 reduce-scatter.2.cloned.1.call-update
  33.8 0.0 all-gather.8.cloned.1.call-start
  33.9 0.0 all-gather.6.cloned.1.call-done
  33.9 4.5 %gather_fusion.1 = f32[2,512,512]{2,1,0:T(8,128)} fusion(f32[4,512,512]{2,1,0:T(8,128)} %all-gather.6.cloned.1.call-done, s32[1024]{0:T(1024)S(1)} %pad_clamp_fusion), kind=kCustom, calls=%fused_computation.clone | custom fusion | bytes 4194312 | tf_op jit(solution)/shard_map/jit(_take)/gather | solution.py:33
  38.5 0.0 copy-start.6
  38.5 0.0 copy-start.4
  38.5 0.0 copy-start.5
  38.5 0.0 copy-start.2
  38.5 3.2 %select_convert_fusion = bf16[2,512,512]{2,1,0:T(8,128)(2,1)} fusion(f32[2,512,512]{2,1,0:T(8,128)} %gather_fusion.1, pred[2]{0:T(512)(128)(4,1)S(1)} %get-tuple-element.29), kind=kLoop, calls=%fused_computation.23 | loop fusion | flops 524288 | bytes 3145730 | tf_op jit(solution)/shard_map/convert_element_type | solution.py:44
  41.6 0.0 all-gather.8.cloned.1.call-update
  41.7 0.0 copy-done.6
  41.7 0.6 dynamic-slice
  42.9 0.0 copy-done.4
  42.9 0.2 dynamic-update-slice.1
  43.2 0.0 copy-done.5
  43.2 0.2 dynamic-update-slice
  43.4 2.6 all-reduce.2
  46.0 0.6 gather_fusion.3
  46.7 0.6 gather_fusion.2
  47.3 0.0 copy-done.2
  47.3 0.1 fusion.14
  47.4 0.6 copy.20
  48.1 0.0 all-gather.10.cloned.1.call-done
  48.1 4.2 %gather_fusion.4 = f32[2,512,512]{2,1,0:T(8,128)} fusion(f32[4,512,512]{2,1,0:T(8,128)} %all-gather.10.cloned.1.call-done, s32[1024]{0:T(1024)S(1)} %pad_clamp_fusion), kind=kCustom, calls=%fused_computation.2.clone | custom fusion | bytes 4194312 | tf_op jit(solution)/shard_map/jit(_take)/gather | solution.py:33
  52.3 7.4 %all-gather.12.cloned.1.call-done = f32[4,512,512]{2,1,0:T(8,128)} async-done(((f32[2,512,512]{2,1,0:T(8,128)}), f32[4,512,512]{2,1,0:T(8,128)}) %all-gather.12.cloned.1.call-update) | async-done | bytes 4194320 | tf_op jit(solution)/shard_map/all_gather | solution.py:26
  59.6 4.2 %gather_fusion.5 = f32[2,512,512]{2,1,0:T(8,128)} fusion(f32[4,512,512]{2,1,0:T(8,128)} %all-gather.12.cloned.1.call-done, s32[1024]{0:T(1024)S(1)} %pad_clamp_fusion), kind=kCustom, calls=%fused_computation.3.clone | custom fusion | bytes 4194312 | tf_op jit(solution)/shard_map/jit(_take)/gather | solution.py:33
  63.8 198.7 %reduce-scatter.2.cloned.1.call-done = bf16[512,2,512]{2,0,1:T(8,128)(2,1)} async-done(((bf16[4096,2,512]{2,0,1:T(8,128)(2,1)}), bf16[512,2,512]{2,0,1:T(8,128)(2,1)}) %reduce-scatter.2.cloned.1.call-update) | async-done | bytes 1048592 | tf_op jit(solution)/shard_map/reduce_scatter | solution.py:54
  262.6 6.9 %divide_subtract_fusion = (f32[2,512,512]{2,1,0:T(8,128)}, f32[2,512,512]{2,1,0:T(8,128)}, f32[2,512,512]{2,1,0:T(8,128)}) fusion(f32[2,512,512]{2,1,0:T(8,128)} %gather_fusion.1, f32[2]{0:T(128)S(1)} %get-tuple-element.31, pred[2]{0:T(512)(128)(4,1)S(1)} %get-tuple-element.29, bf16[512,2,512]{2,0,1:T(8,128)(2,1)} %reduce-scatter.2.cloned.1.call-done, ...), kind=kLoop, calls=%fused_computation.22 | loop fusion | flops 7864320 | bytes 13631514 | tf_op jit(solution)/shard_map/sub | solution.py:68
  269.5 0.0 all-gather.8.cloned.1.call-done
  269.5 13.0 %multiply_convert_fusion.1 = bf16[2,768,512]{2,1,0:T(8,128)(2,1)} fusion(bf16[2,4096,512]{2,1,0:T(8,128)(2,1)} %all-gather.8.cloned.1.call-done, bf16[2,768,4096]{2,1,0:T(8,128)(2,1)} %param.20, f32[2,4096]{1,0:T(2,128)S(1)} %broadcast_select_fusion, f32[2,768]{1,0:T(2,128)S(1)} %add_rsqrt_fusion), kind=kOutput, calls=%fused_computation.16 | convolution fusion | flops 6469189632 | bytes 22583296 | tf_op jit(solution)/shard_map/rtd,rdk->rtk/dot_general | solution.py:47
  (6 shorter events, 0.0 us)
Async XLA Ops:
  8.0 12.2 %copy-start = (bf16[2,768,512]{2,1,0:T(8,128)(2,1)S(1)}, bf16[2,768,512]{2,1,0:T(8,128)(2,1)}, u32[]{:S(2)}) copy-start(bf16[2,768,512]{2,1,0:T(8,128)(2,1)} %param.21) | copy-start | bytes 4718596
  8.0 25.9 %all-gather.6.cloned.1.call-start = ((), (), s32[]{:S(2)}) async-start(), calls=%async_computation.1 | async-start | bytes 6291456 | tf_op jit(solution)/shard_map/all_gather | solution.py:24
  8.7 1.6 copy-start.1
  8.8 3.6 %copy-start.3 = (s32[4]{0:T(128)S(1)}, s32[4]{0:T(128)}, u32[]{:S(2)}) copy-start(s32[4]{0:T(128)} %param.22) | copy-start | bytes 52
  8.8 39.3 %all-gather.10.cloned.1.call-start = ((), (), s32[]{:S(2)}) async-start(), calls=%async_computation.3 | async-start | bytes 6291456 | tf_op jit(solution)/shard_map/all_gather | solution.py:25
  9.5 50.1 %all-gather.12.cloned.1.call-start = ((), (), s32[]{:S(2)}) async-start(), calls=%async_computation.5 | async-start | bytes 6291456 | tf_op jit(solution)/shard_map/all_gather | solution.py:26
  10.3 252.3 %reduce-scatter.2.cloned.1.call-start = ((), (), s32[]{:S(2)}) async-start(), calls=%async_computation.4 | async-start | bytes 9437184 | tf_op jit(solution)/shard_map/reduce_scatter | solution.py:54
  33.8 235.6 %all-gather.8.cloned.1.call-start = ((), (), s32[]{:S(2)}) async-start(), calls=%async_computation.2 | async-start | bytes 9437184 | tf_op jit(solution)/shard_map/all_gather | solution.py:50
  38.5 3.2 %copy-start.6 = (u32[32]{0:T(128)S(1)}, u32[32]{0:T(128)}, u32[]{:S(2)}) copy-start(u32[32]{0:T(128)} %constant.81) | copy-start | bytes 388
  38.5 4.5 %copy-start.4 = (f32[2]{0:T(128)S(1)}, f32[2]{0:T(128)}, u32[]{:S(2)}) copy-start(f32[2]{0:T(128)} %param.19) | copy-start | bytes 28
  38.5 4.7 %copy-start.5 = (f32[2]{0:T(128)S(1)}, f32[2]{0:T(128)}, u32[]{:S(2)}) copy-start(f32[2]{0:T(128)} %param.18) | copy-start | bytes 28
  38.5 8.8 %copy-start.2 = (s32[4,2]{0,1:T(2,128)S(1)}, s32[4,2]{0,1:T(2,128)}, u32[]{:S(2)}) copy-start(s32[4,2]{0,1:T(2,128)} %param.23) | copy-start | bytes 100
Sparse Core Ops, SparseCore 0:
  10.4 16.3 all-gather.5
  28.3 14.8 all-gather.9
  44.8 14.8 all-gather.11
  62.2 155.7 all-gather.7
Sparse Core Ops, SparseCore 1:
  33.9 228.6 reduce-scatter.1
where the time goes:
time: 290 us
  waiting for transfers between devices  208 us (72%)
  matrix products  26.7 us (9%)
  other arithmetic  17.4 us (6%)
  local copies, waits for them, and re-layouts  16.6 us (6%)
  between operations  16 us (6%)
  blocking collectives  4.59 us (2%)
    reduce_scatter x1, waiting for transfers between devices, per_device(): lax.psum_scatter((jnp.einsum('rtd,rtk->drk', columns, cotangent, preferre...  199 us
    gather x6, local copies, waits for them, and re-layouts, per_device(): jnp.take(member, source, axis=0)  14.8 us
    dot_general x1, matrix products, per_device(): jnp.einsum('rtd,rtk->drk', columns, cotangent, preferred_element_type=jnp...  13.6 us
    dot_general x1, matrix products, per_device(): jnp.einsum('rtd,rdk->rtk', columns, lax.all_gather(wide, 'shard', axis=1,...  13 us
    all_gather x1, waiting for transfers between devices, per_device(): lax.all_gather(second_moment, 'run', axis=0, tiled=True)  7.38 us
    reduce_sum x1, other arithmetic, per_device(): square = jnp.mean(values * values, axis=-1, keepdims=True)  7.07 us
    sub x1, other arithmetic, per_device(): taken_weight - rate[:, None, None] * new_first / (jnp.sqrt(new_second) +...  6.9 us
  transfers between devices with their start and end apart: 5, of which 2 were waited for; matrix products, arithmetic and copies ran while one was open for 16% of the time, Pallas kernels for 0%

commit v1 on v0

v1 whole, which is shorter than its diff:
```python
import functools

import jax
import jax.numpy as jnp
from jax import lax
from jax.experimental import pallas as pl
from jax.experimental.pallas import tpu as pltpu
from jax.sharding import PartitionSpec as P

MESH = pl.DeviceIdType.MESH
F32 = jnp.float32
BF16 = jnp.bfloat16
AHEAD = 3


def visit_order(planes):
    return [sorted(range(planes), key=lambda d: (-abs(d - z), -d)) for z in range(planes)]


def exchange_kernel(
    n,
    pick_ref,
    mine_ref,
    x_hbm,
    cot_hbm,
    w_hbm,
    f_hbm,
    s_hbm,
    side_hbm,
    keys_hbm,
    grad_hbm,
    w_out,
    f_out,
    s_out,
    side_out,
    x,
    cot,
    inv,
    w4,
    side4,
    ysend,
    yrecv,
    zrecv,
    gmine,
    gother,
    acc,
    tmp,
    in_sem,
    own_sem,
    out_sem,
    st_send,
    st_recv,
    y_send,
    y_recv,
    z_send,
    z_recv,
    ay_send,
    up_send,
    dn_send,
    ag_recv,
    co_send,
    co_recv,
):
    planes = n // 2
    steps = 2 * planes
    runs, tokens, features = x.shape
    rows = features // n
    width = cot.shape[2]
    core = lax.axis_index("run")
    me = lax.axis_index("shard")
    z = me // 2
    y = me % 2
    orders = visit_order(planes)

    def order_of(s):
        d = jnp.int32(0)
        for a in range(planes):
            for b in range(planes):
                hit = jnp.where(z == a, 1, 0) * jnp.where(s == b, 1, 0)
                d = d + hit * orders[a][b]
        return d

    to_core = {"run": 1 - core}
    to_y = {"shard": z * 2 + 1 - y}
    to_up = {"shard": jnp.minimum(me + 2, n - 1)}
    to_dn = {"shard": jnp.maximum(me - 2, 0)}
    above = z < planes - 1
    below = z > 0

    def load(r):
        return pltpu.make_async_copy(x_hbm.at[r], x.at[r], in_sem.at[r])

    load_cot = pltpu.make_async_copy(cot_hbm, cot, in_sem.at[2])
    load_w = pltpu.make_async_copy(w_hbm, w4.at[pl.ds(0, 2)], in_sem.at[3])
    load_side = pltpu.make_async_copy(side_hbm, side4.at[pl.ds(0, 2)], in_sem.at[4])
    own_f = pltpu.make_async_copy(f_hbm, f_out.at[pl.ds(0, 2)], own_sem.at[0])
    own_s = pltpu.make_async_copy(s_hbm, s_out.at[pl.ds(0, 2)], own_sem.at[1])

    load(0).start()
    load_cot.start()
    load_w.start()
    load_side.start()
    load(1).start()

    barrier = pltpu.get_barrier_semaphore()
    pl.semaphore_signal(barrier, inc=1, device_id=to_core, device_id_type=MESH)
    pl.semaphore_signal(barrier, inc=1, device_id=to_y, device_id_type=MESH)

    @pl.when(above)
    def _():
        pl.semaphore_signal(barrier, inc=1, device_id=to_up, device_id_type=MESH)

    @pl.when(below)
    def _():
        pl.semaphore_signal(barrier, inc=1, device_id=to_dn, device_id_type=MESH)

    pl.semaphore_wait(barrier, 2 + jnp.where(above, 1, 0) + jnp.where(below, 1, 0))

    def remote(src, dst, send, recv, where):
        return pltpu.make_async_remote_copy(
            src_ref=src, dst_ref=dst, send_sem=send, recv_sem=recv, device_id=where, device_id_type=MESH
        )

    far = pl.ds(2, 2)
    state = [
        remote(w_hbm, w4.at[far], st_send.at[0], st_recv.at[0], to_core),
        remote(side_hbm, side4.at[far], st_send.at[1], st_recv.at[1], to_core),
        remote(f_hbm, f_out.at[far], st_send.at[2], st_recv.at[2], to_core),
        remote(s_hbm, s_out.at[far], st_send.at[3], st_recv.at[3], to_core),
    ]
    state[0].start()
    state[1].start()

    def y_copy(k):
        return remote(ysend.at[k], yrecv.at[k], y_send.at[k], y_recv.at[k], to_y)

    def columns(shard):
        return pl.ds(pl.multiple_of(shard * rows, rows), rows)

    def share(r, shard):
        return lax.dot_general(
            x[r, :, columns(shard)], cot[r], (((0,), (0,)), ((), ())), preferred_element_type=F32
        )

    def scale_tokens(r):
        def body(i, carry):
            at = pl.ds(pl.multiple_of(i * 16, 16), 16)
            v = x[r, at, :].astype(F32)
            q = lax.rsqrt(jnp.sum(v * v, axis=-1, keepdims=True) * (1.0 / features) + 1e-05)
            inv[r, at, :] = q
            cot[r, at, :] = (cot[r, at, :].astype(F32) * q).astype(BF16)
            return carry

        lax.fori_loop(0, tokens // 16, body, 0)

    def send_y(k):
        d = order_of(k // 2)
        ysend[k] = share(k % 2, d * 2 + 1 - y).astype(BF16)
        y_copy(k).start()

    def z_copy(k):
        d = order_of(k // 2)
        r = k % 2
        up = d > z
        slot = jnp.where(d == z - 1, 2 * planes + r, d * 2 + r)
        to = jnp.where(up, jnp.minimum(z + 1, planes - 1), jnp.maximum(z - 1, 0)) * 2 + y
        return remote(yrecv.at[k], zrecv.at[slot], z_send.at[k], z_recv.at[slot], {"shard": to})

    def z_wait(slot):
        remote(zrecv.at[slot], zrecv.at[slot], z_send.at[0], z_recv.at[slot], to_y).wait_recv()

    def grad_copy(r):
        return pltpu.make_async_copy(tmp.at[r], grad_hbm.at[r], out_sem.at[r])

    def sum_step(k):
        s = k // 2
        r = k % 2
        d = order_of(s)
        total = share(r, d * 2 + y)
        y_copy(k).wait_recv()
        tmp[r] = total + yrecv[k].astype(F32)
        slot = d * 2 + r
        from_below = jnp.logical_and(d >= z, below)
        from_above = jnp.logical_and(d < z, above)

        @pl.when(jnp.logical_or(from_below, from_above))
        def _():
            z_wait(slot)
            tmp[r] += zrecv[slot].astype(F32)

        @pl.when(s < planes - 1)
        def _():
            yrecv[k] = tmp[r].astype(BF16)
            z_copy(k).start()

        @pl.when(s == planes - 1)
        def _():
            @pl.when(above)
            def _():
                z_wait(2 * planes + r)
                tmp[r] += zrecv[2 * planes + r].astype(F32)

            grad_copy(r).start()

    def ag_copy(shard, sem, to):
        return remote(gmine.at[shard], gmine.at[shard], sem, ag_recv.at[shard], to)

    def core_copy(shard):
        return remote(gmine.at[shard], gother.at[shard], co_send.at[shard], co_recv.at[shard], to_core)

    def hand_on(shard, go_up, go_dn):
        @pl.when(go_up)
        def _():
            ag_copy(shard, up_send.at[shard], to_up).start()

        @pl.when(go_dn)
        def _():
            ag_copy(shard, dn_send.at[shard], to_dn).start()

        core_copy(shard).start()

    def sources(i):
        h = i // 2
        o = i % 2
        yy = jnp.where(o == 0, y, 1 - y)
        lower = jnp.maximum(z - h, 0) * 2 + yy
        upper = jnp.minimum(z + h, planes - 1) * 2 + yy
        has_upper = jnp.logical_and(h > 0, z + h < planes)
        return h, lower, z - h >= 0, upper, has_upper

    def gather_step(i):
        h, lower, has_lower, upper, has_upper = sources(i)

        @pl.when(has_lower)
        def _():
            ag_copy(lower, ay_send.at[0], to_y).wait_recv()
            hand_on(lower, above, jnp.logical_and(h == 0, below))

        @pl.when(has_upper)
        def _():
            ag_copy(upper, ay_send.at[0], to_y).wait_recv()
            hand_on(upper, False, below)

    def use(shard):
        core_copy(shard).wait_recv()

        def body(r, carry):
            keep = mine_ref[pl.ds(r, 1), :]
            w = gmine[shard].astype(F32) * keep + gother[shard].astype(F32) * (1.0 - keep)
            acc[r] += jnp.dot(x[r, :, columns(shard)], w.astype(BF16), preferred_element_type=F32)
            return carry

        lax.fori_loop(0, runs, body, 0)

    def use_step(i):
        _, lower, has_lower, upper, has_upper = sources(i)

        @pl.when(has_lower)
        def _():
            use(lower)

        @pl.when(has_upper)
        def _():
            use(upper)

    load_cot.wait()
    load(0).wait()
    scale_tokens(0)
    send_y(0)

    load_w.wait()
    load_side.wait()
    state[0].wait_recv()
    state[1].wait_recv()
    pick = pick_ref[0]
    gain = side4[pick, 0:rows, :]
    for q in range(width // 128):
        cut = slice(q * 128, (q + 1) * 128)
        gmine[me, :, cut] = (w4[pick, :, cut] * gain).astype(BF16)
    ag_copy(me, ay_send.at[0], to_y).start()
    hand_on(me, above, below)
    state[2].start()
    state[3].start()
    own_f.start()
    own_s.start()
    put_w = pltpu.make_async_copy(w4, w_out, own_sem.at[2])
    put_side = pltpu.make_async_copy(side4, side_out, own_sem.at[3])
    put_w.start()
    put_side.start()

    load(1).wait()
    scale_tokens(1)
    acc[...] = jnp.zeros_like(acc)

    def step(t, carry):
        @pl.when(t < steps)
        def _():
            send_y(t)

        k = t - AHEAD

        @pl.when(k >= 0)
        def _():
            sum_step(k)

            @pl.when(k + 1 < steps)
            def _():
                gather_step(k + 1)

            use_step(k)

        return carry

    lax.fori_loop(1, steps + AHEAD, step, 0)

    def finish(i, carry):
        r = i // (tokens // 16)
        at = pl.ds(pl.multiple_of((i % (tokens // 16)) * 16, 16), 16)
        cot[r, at, :] = (acc[r, at, :] * (inv[r, at, :] * features ** (-0.5))).astype(BF16)
        return carry

    lax.fori_loop(0, runs * (tokens // 16), finish, 0)
    put_keys = pltpu.make_async_copy(cot, keys_hbm, out_sem.at[2])
    put_keys.start()

    def drain(k, carry):
        y_copy(k).wait_send()

        @pl.when(k < steps - 2)
        def _():
            z_copy(k).wait_send()

        return carry

    lax.fori_loop(0, steps, drain, 0)
    ag_copy(me, ay_send.at[0], to_y).wait_send()

    def drain_gather(shard, carry):
        core_copy(shard).wait_send()

        @pl.when(jnp.logical_and(above, shard // 2 <= z))
        def _():
            ag_copy(shard, up_send.at[shard], to_up).wait_send()

        @pl.when(jnp.logical_and(below, shard // 2 >= z))
        def _():
            ag_copy(shard, dn_send.at[shard], to_dn).wait_send()

        return carry

    lax.fori_loop(0, n, drain_gather, 0)
    for copy in state:
        copy.wait_send()
    state[2].wait_recv()
    state[3].wait_recv()
    own_f.wait()
    own_s.wait()
    put_w.wait()
    put_side.wait()
    put_keys.wait()
    grad_copy(0).wait()
    grad_copy(1).wait()


def exchange(n, pick, mine, inputs, cotangent, weight, first, second, side):
    runs, tokens, features = inputs.shape
    rows, width = weight.shape[1:]
    steps = n
    dma = pltpu.SemaphoreType.DMA
    any_spec = pl.BlockSpec(memory_space=pl.ANY)
    four = jax.ShapeDtypeStruct((2 * runs, rows, width), F32)
    return pl.pallas_call(
        functools.partial(exchange_kernel, n),
        out_shape=(
            jax.ShapeDtypeStruct((runs, tokens, width), BF16),
            jax.ShapeDtypeStruct((runs, rows, width), F32),
            four,
            four,
            four,
            jax.ShapeDtypeStruct((2 * runs,) + side.shape[1:], F32),
        ),
        in_specs=[
            pl.BlockSpec(memory_space=pltpu.SMEM),
            pl.BlockSpec(memory_space=pltpu.VMEM),
        ]
        + [any_spec] * 6,
        out_specs=(any_spec,) * 6,
        scratch_shapes=[
            pltpu.VMEM((runs, tokens, features), BF16),
            pltpu.VMEM((runs, tokens, width), BF16),
            pltpu.VMEM((runs, tokens, 1), F32),
            pltpu.VMEM((2 * runs, rows, width), F32),
            pltpu.VMEM((2 * runs,) + side.shape[1:], F32),
            pltpu.VMEM((steps, rows, width), BF16),
            pltpu.VMEM((steps, rows, width), BF16),
            pltpu.VMEM((steps + 2, rows, width), BF16),
            pltpu.VMEM((n, rows, width), BF16),
            pltpu.VMEM((n, rows, width), BF16),
            pltpu.VMEM((runs, tokens, width), F32),
            pltpu.VMEM((runs, rows, width), F32),
            dma((5,)),
            dma((4,)),
            dma((3,)),
            dma((4,)),
            dma((4,)),
            dma((steps,)),
            dma((steps,)),
            dma((steps,)),
            dma((steps + 2,)),
            dma((1,)),
            dma((n,)),
            dma((n,)),
            dma((n,)),
            dma((n,)),
            dma((n,)),
        ],
        compiler_params=pltpu.CompilerParams(
            collective_id=0, has_side_effects=True, vmem_limit_bytes=60 * 1024 * 1024
        ),
        cost_estimate=pl.CostEstimate(
            flops=4 * runs * tokens * features * width, bytes_accessed=40_000_000, transcendentals=0
        ),
        name="exchange",
    )(pick, mine, inputs, cotangent, weight, first, second, side)


def update_kernel(source_ref, factor_ref, grad, w, f, s, side, new_w, new_f, new_s, hyper, *, rows, scale):
    r = pl.program_id(0)
    j = pl.program_id(1)
    height, width = grad.shape[1:]
    tile = lambda v: jnp.concatenate([v] * (width // 128), axis=1)
    gain = side[0, pl.ds(pl.multiple_of(j * height, 8), height), :] * scale
    rate = side[0, rows : rows + 1, :] * factor_ref[r, 0]
    beta = 1.0 - (1.0 - side[0, rows + 1 : rows + 2, :]) * factor_ref[r, 1]

    @pl.when(j == 0)
    def _():
        at = lax.broadcasted_iota(jnp.int32, (1, 2), 1)
        hyper[pl.ds(r, 1), :] = jnp.where(at == 0, rate[:, :2], beta[:, :2])

    rate, beta = tile(rate), tile(beta)
    g = grad[0] * tile(gain)
    first = beta * f[0] + (1.0 - beta) * g
    second = 0.95 * s[0] + 0.05 * g * g
    new_f[0] = first
    new_s[0] = second
    new_w[0] = w[0] - rate * first / (jnp.sqrt(second) + 1e-08)


def update(source, factor, grad, w4, f4, s4, side4, scale):
    runs, rows, width = grad.shape
    height = min(256, rows)
    own = pl.BlockSpec((1, height, width), lambda r, j, src: (r, j, 0))
    taken = pl.BlockSpec((1, height, width), lambda r, j, src: (src[r], j, 0))
    out = jax.ShapeDtypeStruct(grad.shape, F32)
    return pl.pallas_call(
        functools.partial(update_kernel, rows=rows, scale=scale),
        out_shape=(out, out, out, jax.ShapeDtypeStruct((runs, 2), F32)),
        grid_spec=pltpu.PrefetchScalarGridSpec(
            num_scalar_prefetch=1,
            grid=(runs, rows // height),
            in_specs=[
                pl.BlockSpec(memory_space=pltpu.SMEM),
                own,
                taken,
                taken,
                taken,
                pl.BlockSpec((1,) + side4.shape[1:], lambda r, j, src: (src[r], 0, 0)),
            ],
            out_specs=(own, own, own, pl.BlockSpec((runs, 2), lambda r, j, src: (0, 0))),
        ),
        compiler_params=pltpu.CompilerParams(vmem_limit_bytes=40 * 1024 * 1024),
        name="update",
    )(source, factor, grad, w4, f4, s4, side4)


def per_device(
    n,
    weight,
    first_moment,
    second_moment,
    norm_gain,
    learning_rate,
    momentum,
    inputs,
    cotangent,
    winner,
    perturb,
):
    runs, rows, width = weight.shape
    features = inputs.shape[2]
    core = lax.axis_index("run")
    shard = lax.axis_index("shard")
    offset = core * runs
    everyone = jnp.arange(winner.shape[0], dtype=jnp.int32)
    mine = offset + jnp.arange(runs, dtype=jnp.int32)
    named = winner == everyone
    low = jnp.min(jnp.where(named, everyone, winner.shape[0]))
    high = jnp.max(jnp.where(named, everyone, -1))
    chosen = jnp.where(core == 0, low, high)

    def place(run):
        return jnp.where(run // runs == core, run % runs, runs + run % runs).astype(jnp.int32)

    source = lax.dynamic_slice(winner, (offset,), (runs,))
    codes = lax.dynamic_slice(perturb, (offset, jnp.int32(0)), (runs, 2))
    factor = jnp.where(codes == 0, F32(0.8), F32(1.25))
    factor = jnp.where((source != mine)[:, None], factor, F32(1.0))
    gain = lax.dynamic_slice(norm_gain, (jnp.int32(0), shard * rows), (runs, rows))
    side = jnp.concatenate(
        [gain, learning_rate[:, None], momentum[:, None], jnp.zeros((runs, 6), F32)], axis=1
    )
    side = jnp.broadcast_to(side[:, :, None], side.shape + (128,))
    same = jnp.broadcast_to((source == chosen).astype(F32)[:, None], (runs, width))
    keys, grad, w4, f4, s4, side4 = exchange(
        n, place(chosen)[None], same, inputs, cotangent, weight, first_moment, second_moment, side
    )
    new_weight, new_first, new_second, new_hyper = update(
        place(source), factor, grad, w4, f4, s4, side4, features ** (-0.5)
    )
    return (keys, new_weight, new_first, new_second, new_hyper)


def solution(mesh):
    rows = P(("group", "run"), "shard", None)
    placed = (
        rows,
        rows,
        rows,
        P(("group", "run"), None),
        P(("group", "run")),
        P(("group", "run")),
        rows,
        rows,
        P("group"),
        P("group", None),
    )
    return jax.shard_map(
        functools.partial(per_device, mesh.shape["shard"]),
        mesh=mesh,
        in_specs=placed,
        out_specs=(rows, rows, rows, rows, P(("group", "run"), None)),
        check_vma=False,
    )
```

time: 290 us -> 163 us (0.56)
  waiting for transfers between devices: 208 us -> 0 us
  Pallas kernels: 0 us -> 145 us
  matrix products: 26.7 us -> 0 us
  other arithmetic: 17.4 us -> 2.93 us
  between operations: 16 us -> 2.01 us
  blocking collectives: 4.59 us -> 0 us
  local copies, waits for them, and re-layouts: 16.6 us -> 12.4 us
    reduce_scatter x1 -> x0, waiting for transfers between devices: 199 us -> none  [per_device(): lax.psum_scatter((jnp.einsum('rtd,rtk->drk', columns, cotangent, preferre...]
    pallas_call x0 -> x2, Pallas kernels: none -> 145 us  [the longest x1 140 us: exchange(): pl.pallas_call(functools.partial(exchange_kernel, n), out_shape=(jax.Shap...]
    dot_general x2 -> x0, matrix products: 26.7 us -> none  [the longest x1 13.6 us: per_device(): jnp.einsum('rtd,rtk->drk', columns, cotangent, preferred_element_type=jnp...]
    gather x6 -> x0, local copies, waits for them, and re-layouts: 14.8 us -> none  [per_device(): jnp.take(member, source, axis=0)]
    all_gather x4 -> x0, waiting for transfers between devices: 7.4 us -> none  [the longest x1 7.38 us: per_device(): lax.all_gather(second_moment, 'run', axis=0, tiled=True)]
    reduce_sum x1 -> x0, other arithmetic: 7.07 us -> none  [per_device(): square = jnp.mean(values * values, axis=-1, keepdims=True)]
    sub x2 -> x0, other arithmetic: 6.91 us -> none  [the longest x1 6.9 us: per_device(): taken_weight - rate[:, None, None] * new_first / (jnp.sqrt(new_second) +...]
    unnamed x21 -> x14, local copies, waits for them, and re-layouts: 1.79 us -> 8.44 us
  transfers between devices with their start and end apart: 5 -> 0, of which waited for: 2 -> 0; matrix products, arithmetic and copies ran while one was open for 16% -> 0% of each run, Pallas kernels for 0% -> 0%
where the time goes in v1:
time: 163 us
  Pallas kernels  145 us (89%)
  local copies, waits for them, and re-layouts  12.4 us (8%)
  other arithmetic  2.93 us (2%)
  between operations  2.01 us (1%)
    pallas_call x1, Pallas kernels, exchange(): pl.pallas_call(functools.partial(exchange_kernel, n), out_shape=(jax.Shap...  140 us
    unnamed x14, local copies, waits for them, and re-layouts  8.44 us
    pallas_call x1, Pallas kernels, update(): pl.pallas_call(functools.partial(update_kernel, rows=rows, scale=scale),...  5.49 us

profile of v1, /device:TPU:0, one launch (start us, length us, event | category | flops | bytes accessed | tf_op | source)
XLA Modules:
  0.0 162.5 jit_solution(13342404833068939881)
XLA Ops:
  0.6 0.0 copy-start
  0.7 0.7 compare_select_fusion.1.source_ref
  1.4 0.7 copy.15
  2.1 0.7 copy.16
  2.9 0.7 constant_dynamic-slice_fusion
  3.6 0.1 copy.18
  3.7 1.3 select_reduce_fusion
  6.4 0.7 add_compare_fusion
  7.1 0.1 fusion.factor_ref
  7.2 0.1 pad.3.clone
  7.2 0.0 copy-done
  7.3 0.1 maximum_maximum_fusion
  7.3 0.7 broadcast_in_dim.52.mine_ref
  8.0 1.0 broadcast_in_dim.55.side_hbm
  9.0 139.7 %exchange.1 = (bf16[2,768,512]{2,1,0:T(8,128)(2,1)}, f32[2,512,512]{2,1,0:T(8,128)}, f32[4,512,512]{2,1,0:T(8,128)}, f32[4,512,512]{2,1,0:T(8,128)}, f32[4,512,512]{2,1,0:T(8,128)}, /*index=5*/f32[4,520,128]{2,1,0:T(8,128)}) custom-call(s32[1]{0:T(128)} %bitcast.pick_ref, f32[2,512]{1,0:T(2,128)} %broadcast_in_dim.52.mine_ref, bf16[2,768,4096]{2,1,0:T(8,128)(2,1)} %x_hbm.1, ...), custom_call_target="tpu_custom_call" | custom-call | flops 12884901888 | bytes 40000000 | tf_op jit(solution)/shard_map/exchange/pallas_call | solution.py:372
  148.7 0.0 copy-start.1
  148.7 2.2 %copy-done.1 = f32[4,512,512]{2,1,0:T(8,128)S(1)} copy-done((f32[4,512,512]{2,1,0:T(8,128)S(1)}, f32[4,512,512]{2,1,0:T(8,128)}, u32[]{:S(2)}) %copy-start.1) | copy-done | bytes 4194328
  150.9 0.0 copy-start.2
  150.9 2.2 %copy-done.2 = f32[4,512,512]{2,1,0:T(8,128)S(1)} copy-done((f32[4,512,512]{2,1,0:T(8,128)S(1)}, f32[4,512,512]{2,1,0:T(8,128)}, u32[]{:S(2)}) %copy-start.2) | copy-done | bytes 4194328
  153.1 0.0 copy-start.3
  153.1 1.6 copy-done.3
  154.7 0.0 copy-start.4
  154.7 1.2 copy-done.4
  155.9 0.0 copy-start.5
  155.9 5.5 %update.1 = (f32[2,512,512]{2,1,0:T(8,128)}, f32[2,512,512]{2,1,0:T(8,128)}, f32[2,512,512]{2,1,0:T(8,128)}, f32[2,2]{1,0:T(2,128)}) custom-call(s32[2]{0:T(128)S(1)} %compare_select_fusion.1.source_ref, f32[2,2]{1,0:T(2,128)S(1)} %fusion.factor_ref, f32[2,512,512]{2,1,0:T(8,128)S(1)} %copy-done.3, f32[4,512,512]{2,1,0:T(8,128)S(1)} %copy-done.1, ...), custom_call_target="tpu_custom_call" | custom-call | tf_op jit(solution)/shard_map/update/pallas_call | solution.py:456
  161.4 0.0 copy-done.5
  161.4 1.1 copy.20
  (2 shorter events, 0.0 us)
Async XLA Ops:
  0.6 6.6 %copy-start = (f32[2,4096]{1,0:T(2,128)S(1)}, f32[2,4096]{1,0:T(2,128)}, u32[]{:S(2)}) copy-start(f32[2,4096]{1,0:T(2,128)} %param.13) | copy-start | bytes 98308
  148.7 2.2 %copy-start.1 = (f32[4,512,512]{2,1,0:T(8,128)S(1)}, f32[4,512,512]{2,1,0:T(8,128)}, u32[]{:S(2)}) copy-start(f32[4,512,512]{2,1,0:T(8,128)} %get-tuple-element.17.w) | copy-start | bytes 12582916
  150.9 2.2 %copy-start.2 = (f32[4,512,512]{2,1,0:T(8,128)S(1)}, f32[4,512,512]{2,1,0:T(8,128)}, u32[]{:S(2)}) copy-start(f32[4,512,512]{2,1,0:T(8,128)} %get-tuple-element.18.f) | copy-start | bytes 12582916
  153.1 1.6 copy-start.3
  154.7 1.2 copy-start.4
  155.9 5.5 %copy-start.5 = (bf16[2,768,512]{2,1,0:T(8,128)(2,1)S(1)}, bf16[2,768,512]{2,1,0:T(8,128)(2,1)}, u32[]{:S(2)}) copy-start(bf16[2,768,512]{2,1,0:T(8,128)(2,1)} %get-tuple-element.34) | copy-start | bytes 4718596

commit v2 on v1

--- a/solution.py
+++ b/solution.py
@@ -100,7 +100,6 @@
     load_cot.start()
     load_w.start()
     load_side.start()
-    load(1).start()
 
     barrier = pltpu.get_barrier_semaphore()
     pl.semaphore_signal(barrier, inc=1, device_id=to_core, device_id_type=MESH)
@@ -151,7 +150,7 @@
             cot[r, at, :] = (cot[r, at, :].astype(F32) * q).astype(BF16)
             return carry
 
-        lax.fori_loop(0, tokens // 16, body, 0)
+        lax.fori_loop(0, tokens // 16, body, 0, unroll=4)
 
     def send_y(k):
         d = order_of(k // 2)
@@ -265,6 +264,7 @@
 
     load_cot.wait()
     load(0).wait()
+    load(1).start()
     scale_tokens(0)
     send_y(0)
 
@@ -319,7 +319,7 @@
         cot[r, at, :] = (acc[r, at, :] * (inv[r, at, :] * features ** (-0.5))).astype(BF16)
         return carry
 
-    lax.fori_loop(0, runs * (tokens // 16), finish, 0)
+    lax.fori_loop(0, runs * (tokens // 16), finish, 0, unroll=4)
     put_keys = pltpu.make_async_copy(cot, keys_hbm, out_sem.at[2])
     put_keys.start()
 

time: 163 us -> 161 us (0.988)
  Pallas kernels: 145 us -> 143 us
    pallas_call x1, Pallas kernels: 140 us -> 137 us  [exchange(): pl.pallas_call(functools.partial(exchange_kernel, n), out_shape=(jax.Shap...]
where the time goes in v2:
time: 161 us; the launch traced here: 160 us
  Pallas kernels  143 us (89%)
  local copies, waits for them, and re-layouts  12.4 us (8%)
  other arithmetic  2.93 us (2%)
  between operations  2.01 us (1%)
    pallas_call x1, Pallas kernels, exchange(): pl.pallas_call(functools.partial(exchange_kernel, n), out_shape=(jax.Shap...  137 us
    unnamed x14, local copies, waits for them, and re-layouts  8.44 us
    pallas_call x1, Pallas kernels, update(): pl.pallas_call(functools.partial(update_kernel, rows=rows, scale=scale),...  5.49 us

profile of v2, /device:TPU:0, one launch (start us, length us, event | category | flops | bytes accessed | tf_op | source)
XLA Modules:
  0.0 159.9 jit_solution(10275586272405613051)
XLA Ops:
  0.6 0.0 copy-start
  0.7 0.7 compare_select_fusion.1.source_ref
  1.4 0.7 copy.15
  2.1 0.7 copy.16
  2.9 0.7 constant_dynamic-slice_fusion
  3.6 0.1 copy.18
  3.7 1.3 select_reduce_fusion
  6.4 0.7 add_compare_fusion
  7.1 0.1 fusion.factor_ref
  7.2 0.1 pad.3.clone
  7.2 0.0 copy-done
  7.3 0.1 maximum_maximum_fusion
  7.3 0.7 broadcast_in_dim.52.mine_ref
  8.0 1.0 broadcast_in_dim.55.side_hbm
  9.0 137.1 %exchange.1 = (bf16[2,768,512]{2,1,0:T(8,128)(2,1)}, f32[2,512,512]{2,1,0:T(8,128)}, f32[4,512,512]{2,1,0:T(8,128)}, f32[4,512,512]{2,1,0:T(8,128)}, f32[4,512,512]{2,1,0:T(8,128)}, /*index=5*/f32[4,520,128]{2,1,0:T(8,128)}) custom-call(s32[1]{0:T(128)} %bitcast.pick_ref, f32[2,512]{1,0:T(2,128)} %broadcast_in_dim.52.mine_ref, bf16[2,768,4096]{2,1,0:T(8,128)(2,1)} %x_hbm.1, ...), custom_call_target="tpu_custom_call" | custom-call | flops 12884901888 | bytes 40000000 | tf_op jit(solution)/shard_map/exchange/pallas_call | solution.py:372
  146.1 0.0 copy-start.1
  146.1 2.2 %copy-done.1 = f32[4,512,512]{2,1,0:T(8,128)S(1)} copy-done((f32[4,512,512]{2,1,0:T(8,128)S(1)}, f32[4,512,512]{2,1,0:T(8,128)}, u32[]{:S(2)}) %copy-start.1) | copy-done | bytes 4194328
  148.3 0.0 copy-start.2
  148.3 2.2 %copy-done.2 = f32[4,512,512]{2,1,0:T(8,128)S(1)} copy-done((f32[4,512,512]{2,1,0:T(8,128)S(1)}, f32[4,512,512]{2,1,0:T(8,128)}, u32[]{:S(2)}) %copy-start.2) | copy-done | bytes 4194328
  150.5 0.0 copy-start.3
  150.5 1.6 copy-done.3
  152.1 0.0 copy-start.4
  152.1 1.2 copy-done.4
  153.3 0.0 copy-start.5
  153.3 5.5 %update.1 = (f32[2,512,512]{2,1,0:T(8,128)}, f32[2,512,512]{2,1,0:T(8,128)}, f32[2,512,512]{2,1,0:T(8,128)}, f32[2,2]{1,0:T(2,128)}) custom-call(s32[2]{0:T(128)S(1)} %compare_select_fusion.1.source_ref, f32[2,2]{1,0:T(2,128)S(1)} %fusion.factor_ref, f32[2,512,512]{2,1,0:T(8,128)S(1)} %copy-done.3, f32[4,512,512]{2,1,0:T(8,128)S(1)} %copy-done.1, ...), custom_call_target="tpu_custom_call" | custom-call | tf_op jit(solution)/shard_map/update/pallas_call | solution.py:456
  158.8 0.0 copy-done.5
  158.8 1.1 copy.20
  (2 shorter events, 0.0 us)
Async XLA Ops:
  0.6 6.6 %copy-start = (f32[2,4096]{1,0:T(2,128)S(1)}, f32[2,4096]{1,0:T(2,128)}, u32[]{:S(2)}) copy-start(f32[2,4096]{1,0:T(2,128)} %param.13) | copy-start | bytes 98308
  146.1 2.2 %copy-start.1 = (f32[4,512,512]{2,1,0:T(8,128)S(1)}, f32[4,512,512]{2,1,0:T(8,128)}, u32[]{:S(2)}) copy-start(f32[4,512,512]{2,1,0:T(8,128)} %get-tuple-element.17.w) | copy-start | bytes 12582916
  148.3 2.2 %copy-start.2 = (f32[4,512,512]{2,1,0:T(8,128)S(1)}, f32[4,512,512]{2,1,0:T(8,128)}, u32[]{:S(2)}) copy-start(f32[4,512,512]{2,1,0:T(8,128)} %get-tuple-element.18.f) | copy-start | bytes 12582916
  150.5 1.6 copy-start.3
  152.1 1.2 copy-start.4
  153.3 5.5 %copy-start.5 = (bf16[2,768,512]{2,1,0:T(8,128)(2,1)S(1)}, bf16[2,768,512]{2,1,0:T(8,128)(2,1)}, u32[]{:S(2)}) copy-start(bf16[2,768,512]{2,1,0:T(8,128)(2,1)} %get-tuple-element.34) | copy-start | bytes 4718596
